TPU v7x, 32 devices: a whole 2x2x4 slice. The times are simulated.
32 devices in a mesh: groups: 2 (over y), context: 4 (over z), tensor: 4 (over x, core).
Axes of the slice: x: 2, y: 2, z: 4, core: 2. Of those that a mesh axis runs over, the one named last changes fastest.
Arguments:
- inputs: bfloat16 [4096, 1024], P(('groups', 'context')), parts along dimension 0, may hold values from -6 to 6
- frame_valid: int32 [4096], P(('groups', 'context')), parts along dimension 0, may hold values from 0 to 1, as said below
- norm1_gain: float32 [1024], replicated, may hold values from 0.1 to 1.9
- w_query: bfloat16 [1024, 1024], P(None, 'tensor')
- w_key: bfloat16 [1024, 1024], P(None, 'tensor')
- w_value: bfloat16 [1024, 1024], P(None, 'tensor'), may hold values from -0.1875 to 0.1875
- w_out: bfloat16 [1024, 1024], P('tensor'), may hold values from -0.1875 to 0.1875
- norm2_gain: float32 [1024], replicated, may hold values from 0.1 to 1.9
- w_point1: bfloat16 [2, 1024, 1024], P(None, None, 'tensor'), may hold values from -0.1875 to 0.1875
- w_depth: float32 [31, 1024], P(None, 'tensor'), may hold values from -1.5 to 1.5
- bn_scale: float32 [1024], P('tensor'), may hold values from 0.1 to 1.9
- bn_shift: float32 [1024], P('tensor'), may hold values from -1 to 1
- w_point2: bfloat16 [1024, 1024], P('tensor'), may hold values from -0.1875 to 0.1875
Outputs:
- output: bfloat16 [4096, 1024], P(('groups', 'context', 'tensor')), parts along dimension 0
There are 2 independent parts, one for each index of `groups`. A program takes and returns all parts, laid end to end along the dimension named above; an argument that names none is the same for every part. Nothing has to cross between parts.
Inputs may be any that keep to these rules, and one draw needn't show every extreme that they name: `frame_valid`: the transcript frames form a prefix of the window of at least 1024 frames, followed by at least one padded frame.
All inputs are finite; a program needn't handle non-finite values.
Results may differ from a plain program's by a relative error of at most 0.0095.
Values may be sent and summed in bfloat16 or wider, within the bound.
A program may use at most 64 MiB of HBM per device.

v0:
```python
import math
import jax
import jax.numpy as jnp
from jax import lax
from jax.sharding import PartitionSpec as P

HD = 64
NEG = -1e30


def with_halo(block, sides, width):
    for axis, dim in sides:
        count = lax.axis_size(axis)
        forward = [(i, i + 1) for i in range(count - 1)]
        backward = [(target, source) for source, target in forward]
        low = lax.ppermute(
            lax.slice_in_dim(block, block.shape[dim] - width, None, axis=dim), axis, forward
        )
        high = lax.ppermute(lax.slice_in_dim(block, 0, width, axis=dim), axis, backward)
        block = jnp.concatenate([low, block, high], axis=dim)
    return block


def normalize(rows, gain):
    values = rows.astype(jnp.float32)
    center = jnp.mean(values, axis=-1, keepdims=True)
    spread = jnp.mean(jnp.square(values - center), axis=-1, keepdims=True)
    return ((values - center) * lax.rsqrt(spread + 1e-05) * gain).astype(jnp.bfloat16)


def local(
    inputs,
    frame_valid,
    norm1_gain,
    w_query,
    w_key,
    w_value,
    w_out,
    norm2_gain,
    w_point1,
    w_depth,
    bn_scale,
    bn_shift,
    w_point2,
):
    frames = inputs.shape[0]
    local_cols = w_query.shape[1]
    head_dim = HD
    heads_here = local_cols // head_dim
    scale = 1.0 / math.sqrt(head_dim)
    normed = normalize(inputs, norm1_gain)
    query = jnp.dot(normed, w_query, preferred_element_type=jnp.float32).astype(jnp.bfloat16)
    query = query.reshape(frames, heads_here, head_dim)
    keys = jnp.dot(normed, w_key, preferred_element_type=jnp.float32).astype(jnp.bfloat16)
    vals = jnp.dot(normed, w_value, preferred_element_type=jnp.float32).astype(jnp.bfloat16)

    def update(carry, key_blk, val_blk, valid_blk):
        run_max, run_sum, accum = carry
        rows = key_blk.shape[0]
        key_heads = key_blk.reshape(rows, heads_here, head_dim)
        val_heads = val_blk.reshape(rows, heads_here, head_dim)
        scores = (
            jnp.einsum("qhd,khd->hqk", query, key_heads, preferred_element_type=jnp.float32) * scale
        )
        live = (valid_blk > 0)[None, None, :]
        scores = jnp.where(live, scores, NEG)
        new_max = jnp.maximum(run_max, jnp.max(scores, axis=-1))
        weights = jnp.where(live, jnp.exp(scores - new_max[:, :, None]), 0.0)
        factor = jnp.exp(run_max - new_max)
        run_sum = run_sum * factor + jnp.sum(weights, axis=-1)
        mixed = jnp.einsum(
            "hqk,khd->qhd",
            weights.astype(jnp.bfloat16),
            val_heads,
            preferred_element_type=jnp.float32,
        )
        accum = accum * jnp.repeat(factor.T, head_dim, axis=1) + mixed.reshape(frames, local_cols)
        return (new_max, run_sum, accum)

    def visit(carry, key_blk, val_blk, valid_blk):
        return update(carry, key_blk, val_blk, valid_blk)

    start_state = (
        jnp.full((heads_here, frames), NEG, jnp.float32),
        jnp.zeros((heads_here, frames), jnp.float32),
        jnp.zeros((frames, local_cols), jnp.float32),
    )
    carry = start_state
    key_part = lax.all_gather(keys, "context", axis=0, tiled=True)
    val_part = lax.all_gather(vals, "context", axis=0, tiled=True)
    valid_part = lax.all_gather(frame_valid, "context", axis=0, tiled=True)
    rows = key_part.shape[0]
    shards = max(rows // frames, 1)
    group = math.gcd(shards, max(1536 // frames, 1))
    blocks = shards // group
    block_rows = rows // blocks

    def advance(state, items):
        return (visit(state, items[0], items[1], items[2]), None)

    stacked = (
        key_part.reshape(blocks, block_rows, local_cols),
        val_part.reshape(blocks, block_rows, local_cols),
        valid_part.reshape(blocks, block_rows),
    )
    carry, unused = lax.scan(advance, carry, stacked)
    run_max, run_sum, accum = carry
    attended = (accum / jnp.repeat(run_sum.T, head_dim, axis=1)).astype(jnp.bfloat16)
    share = frames // lax.axis_size("tensor")
    first_row = lax.axis_index("tensor") * share
    total = lax.psum(jnp.dot(attended, w_out, preferred_element_type=jnp.float32), "tensor")
    residual = (inputs.astype(jnp.float32) + total).astype(jnp.bfloat16)
    normed_two = normalize(residual, norm2_gain)
    residual_rows = lax.dynamic_slice_in_dim(residual, first_row, share, 0)
    value_half = jnp.dot(normed_two, w_point1[0], preferred_element_type=jnp.float32)
    gate_half = jnp.dot(normed_two, w_point1[1], preferred_element_type=jnp.float32)
    gated = jnp.where(
        (frame_valid > 0)[:, None], value_half * jax.nn.sigmoid(gate_half), 0.0
    ).astype(jnp.bfloat16)
    taps = w_depth.shape[0]
    half = (taps - 1) // 2
    padded = with_halo(gated, (("context", 0),), half)
    depth = jnp.zeros((frames, gated.shape[1]), jnp.float32)
    for tap in range(taps):
        depth = depth + padded[tap : tap + frames].astype(jnp.float32) * w_depth[tap]
    activated = jax.nn.silu(depth * bn_scale + bn_shift).astype(jnp.bfloat16)
    conv_rows = lax.psum_scatter(
        jnp.dot(activated, w_point2, preferred_element_type=jnp.float32).astype(jnp.bfloat16),
        "tensor",
        scatter_dimension=0,
        tiled=True,
    ).astype(jnp.float32)
    return (residual_rows.astype(jnp.float32) + conv_rows).astype(jnp.bfloat16)


def solution(mesh):
    placed = (
        P(("groups", "context"), None),
        P(("groups", "context")),
        P(),
        P(None, "tensor"),
        P(None, "tensor"),
        P(None, "tensor"),
        P("tensor", None),
        P(),
        P(None, None, "tensor"),
        P(None, "tensor"),
        P("tensor"),
        P("tensor"),
        P("tensor", None),
    )
    return jax.shard_map(
        local,
        mesh=mesh,
        in_specs=placed,
        out_specs=P(("groups", "context", "tensor"), None),
        check_vma=False,
    )
```

profile of v0, /device:TPU:0, one launch (start us, length us, event | category | flops | bytes accessed | tf_op | source)
XLA Modules:
  0.0 218.2 jit_solution(7202695658550756041)
XLA Ops:
  12.5 13.7 %all-gather = s32[4,1,512]{2,1,0:T(1,128)S(1)} all-gather(s32[1,1,512]{2,1,0:T(1,128)S(1)} %bitcast.111), channel_id=1, replica_groups=mesh['groups'=2,'context'=4,'tensor'=4] {'context'}, dimensions={0}, use_global_device_ids=true | all-gather | bytes 10240 | tf_op jit(solution)/shard_map/all_gather | solution.py:91
  26.2 1.7 convolution_convert_fusion.2
  27.9 14.0 %all-gather.4.cloned.1.call-done = bf16[2048,256]{1,0:T(8,128)(2,1)} async-done(((bf16[512,256]{1,0:T(8,128)(2,1)}), bf16[2048,256]{1,0:T(8,128)(2,1)}) %all-gather.4.cloned.1.call-update) | async-done | bytes 1048592 | tf_op jit(solution)/shard_map/all_gather | solution.py:89
  41.9 29.0 %all-gather.6.cloned.1.call-done = bf16[2048,256]{1,0:T(8,128)(2,1)} async-done(((bf16[512,256]{1,0:T(8,128)(2,1)}), bf16[2048,256]{1,0:T(8,128)(2,1)}) %all-gather.6.cloned.1.call-update) | async-done | bytes 1048592 | tf_op jit(solution)/shard_map/all_gather | solution.py:90
  70.9 44.4 %while.15 = (s32[]{:T(128)}, f32[4,512]{1,0:T(4,128)S(1)}, f32[4,512]{1,0:T(4,128)S(1)}, f32[512,256]{0,1:T(8,128)S(1)}, s32[4,512]{1,0:T(4,128)S(1)}, /*index=5...) while((s32[]{:T(128)}, f32[4,512]{1,0:T(4,128)S(1)}, ...), condition=%wide.region_5.6_spmd.clone, body=%wide.region_2.5_spmd.clone.sunk | while | flops 282472960 | bytes 17698944 | solution.py:106
  72.2 2.9 %bitcast_reduce_fusion.2 = (f32[4,512]{1,0:T(4,128)S(1)}, f32[4,512,512]{2,1,0:T(8,128)}) fusion(pred[512]{0:T(512)(128)(4,1)S(1)} %compare_reduce_fusion.2, bf16[512,4,64]{0,2,1:T(8,128)(2,1)S(1)} %bitcast.104, bf16[512,4,64]{0,2,1:T(8,128)(2,1)S(1)} %get-tuple-element.237), kind=kOutput, calls=%fused_computation.1.clone.1 | convolution fusion | flops 137361408 | bytes 4727296 | tf_op jit(solution)/shard_map/while/body/eval_jaxpr/qhd,khd->hqk/dot_general | solution.py:63
  75.1 3.3 %fusion.96 = f32[4,512]{1,0:T(4,128)S(1)} fusion(f32[4,512,512]{2,1,0:T(8,128)} %get-tuple-element.208, f32[4,512]{1,0:T(4,128)S(1)} %get-tuple-element.232, pred[512]{0:T(512)(128)(4,1)S(1)} %compare_reduce_fusion.2), kind=kLoop, calls=%fused_computation.6.clone.1 | loop fusion | flops 5240832 | bytes 4211200 | tf_op jit(solution)/shard_map/while/body/eval_jaxpr/reduce_sum | solution.py:70
  78.6 3.3 %fusion.98 = f32[4,64,512]{2,1,0:T(8,128)S(1)} fusion(bf16[512,4,64]{0,2,1:T(8,128)(2,1)S(1)} %bitcast.106, f32[4,512,512]{2,1,0:T(8,128)} %get-tuple-element.208, f32[4,512]{1,0:T(4,128)S(1)} %get-tuple-element.232, pred[512]{0:T(512)(128)(4,1)S(1)} %compare_reduce_fusion.2), kind=kOutput, calls=%fused_computation.7.clone.1 | convolution fusion | flops 139460608 | bytes 4989440 | tf_op jit(solution)/shard_map/while/body/eval_jaxpr/hqk,khd->qhd/dot_general | solution.py:71
  83.3 2.9 %bitcast_reduce_fusion.2 = (f32[4,512]{1,0:T(4,128)S(1)}, f32[4,512,512]{2,1,0:T(8,128)}) fusion(pred[512]{0:T(512)(128)(4,1)S(1)} %compare_reduce_fusion.2, bf16[512,4,64]{0,2,1:T(8,128)(2,1)S(1)} %bitcast.104, bf16[512,4,64]{0,2,1:T(8,128)(2,1)S(1)} %get-tuple-element.237), kind=kOutput, calls=%fused_computation.1.clone.1 | convolution fusion | flops 137361408 | bytes 4727296 | tf_op jit(solution)/shard_map/while/body/eval_jaxpr/qhd,khd->hqk/dot_general | solution.py:63
  86.2 3.3 %fusion.96 = f32[4,512]{1,0:T(4,128)S(1)} fusion(f32[4,512,512]{2,1,0:T(8,128)} %get-tuple-element.208, f32[4,512]{1,0:T(4,128)S(1)} %get-tuple-element.232, pred[512]{0:T(512)(128)(4,1)S(1)} %compare_reduce_fusion.2), kind=kLoop, calls=%fused_computation.6.clone.1 | loop fusion | flops 5240832 | bytes 4211200 | tf_op jit(solution)/shard_map/while/body/eval_jaxpr/reduce_sum | solution.py:70
  89.7 3.3 %fusion.98 = f32[4,64,512]{2,1,0:T(8,128)S(1)} fusion(bf16[512,4,64]{0,2,1:T(8,128)(2,1)S(1)} %bitcast.106, f32[4,512,512]{2,1,0:T(8,128)} %get-tuple-element.208, f32[4,512]{1,0:T(4,128)S(1)} %get-tuple-element.232, pred[512]{0:T(512)(128)(4,1)S(1)} %compare_reduce_fusion.2), kind=kOutput, calls=%fused_computation.7.clone.1 | convolution fusion | flops 139460608 | bytes 4989440 | tf_op jit(solution)/shard_map/while/body/eval_jaxpr/hqk,khd->qhd/dot_general | solution.py:71
  94.4 2.9 %bitcast_reduce_fusion.2 = (f32[4,512]{1,0:T(4,128)S(1)}, f32[4,512,512]{2,1,0:T(8,128)}) fusion(pred[512]{0:T(512)(128)(4,1)S(1)} %compare_reduce_fusion.2, bf16[512,4,64]{0,2,1:T(8,128)(2,1)S(1)} %bitcast.104, bf16[512,4,64]{0,2,1:T(8,128)(2,1)S(1)} %get-tuple-element.237), kind=kOutput, calls=%fused_computation.1.clone.1 | convolution fusion | flops 137361408 | bytes 4727296 | tf_op jit(solution)/shard_map/while/body/eval_jaxpr/qhd,khd->hqk/dot_general | solution.py:63
  97.3 3.3 %fusion.96 = f32[4,512]{1,0:T(4,128)S(1)} fusion(f32[4,512,512]{2,1,0:T(8,128)} %get-tuple-element.208, f32[4,512]{1,0:T(4,128)S(1)} %get-tuple-element.232, pred[512]{0:T(512)(128)(4,1)S(1)} %compare_reduce_fusion.2), kind=kLoop, calls=%fused_computation.6.clone.1 | loop fusion | flops 5240832 | bytes 4211200 | tf_op jit(solution)/shard_map/while/body/eval_jaxpr/reduce_sum | solution.py:70
  100.8 3.3 %fusion.98 = f32[4,64,512]{2,1,0:T(8,128)S(1)} fusion(bf16[512,4,64]{0,2,1:T(8,128)(2,1)S(1)} %bitcast.106, f32[4,512,512]{2,1,0:T(8,128)} %get-tuple-element.208, f32[4,512]{1,0:T(4,128)S(1)} %get-tuple-element.232, pred[512]{0:T(512)(128)(4,1)S(1)} %compare_reduce_fusion.2), kind=kOutput, calls=%fused_computation.7.clone.1 | convolution fusion | flops 139460608 | bytes 4989440 | tf_op jit(solution)/shard_map/while/body/eval_jaxpr/hqk,khd->qhd/dot_general | solution.py:71
  105.5 2.9 %bitcast_reduce_fusion.2 = (f32[4,512]{1,0:T(4,128)S(1)}, f32[4,512,512]{2,1,0:T(8,128)}) fusion(pred[512]{0:T(512)(128)(4,1)S(1)} %compare_reduce_fusion.2, bf16[512,4,64]{0,2,1:T(8,128)(2,1)S(1)} %bitcast.104, bf16[512,4,64]{0,2,1:T(8,128)(2,1)S(1)} %get-tuple-element.237), kind=kOutput, calls=%fused_computation.1.clone.1 | convolution fusion | flops 137361408 | bytes 4727296 | tf_op jit(solution)/shard_map/while/body/eval_jaxpr/qhd,khd->hqk/dot_general | solution.py:63
  108.4 3.3 %fusion.96 = f32[4,512]{1,0:T(4,128)S(1)} fusion(f32[4,512,512]{2,1,0:T(8,128)} %get-tuple-element.208, f32[4,512]{1,0:T(4,128)S(1)} %get-tuple-element.232, pred[512]{0:T(512)(128)(4,1)S(1)} %compare_reduce_fusion.2), kind=kLoop, calls=%fused_computation.6.clone.1 | loop fusion | flops 5240832 | bytes 4211200 | tf_op jit(solution)/shard_map/while/body/eval_jaxpr/reduce_sum | solution.py:70
  111.9 3.3 %fusion.98 = f32[4,64,512]{2,1,0:T(8,128)S(1)} fusion(bf16[512,4,64]{0,2,1:T(8,128)(2,1)S(1)} %bitcast.106, f32[4,512,512]{2,1,0:T(8,128)} %get-tuple-element.208, f32[4,512]{1,0:T(4,128)S(1)} %get-tuple-element.232, pred[512]{0:T(512)(128)(4,1)S(1)} %compare_reduce_fusion.2), kind=kOutput, calls=%fused_computation.7.clone.1 | convolution fusion | flops 139460608 | bytes 4989440 | tf_op jit(solution)/shard_map/while/body/eval_jaxpr/hqk,khd->qhd/dot_general | solution.py:71
  115.4 1.8 fusion.73
  117.4 50.9 %all-reduce.2.cloned.1.call-done = f32[512,1024]{1,0:T(8,128)} async-done(((f32[512,1024]{1,0:T(8,128)}), f32[512,1024]{1,0:T(8,128)}) %all-reduce.2.cloned.1.call-update) | async-done | bytes 2097168 | tf_op jit(solution)/shard_map/psum | solution.py:111
  168.3 2.0 convert_reduce_fusion.1
  173.2 4.5 %collective-permute-start = (bf16[15,256]{1,0:T(8,128)(2,1)S(1)}, bf16[15,256]{1,0:T(8,128)(2,1)S(1)}, u32[]{:S(2)}, u32[]{:S(2)}) collective-permute-start(bf16[15,256]{1,0:T(8,128)(2,1)S(1)} %get-tuple-element.117), channel_id=1, source_target_pairs={{0,4},{4,8},{8,12},{1,5},{5,9},{9,13},{2,6},{6,10},{10,14},{3,7},{... | collective-permute-start | bytes 23048 | tf_op jit(solution)/shard_map/ppermute | solution.py:16
  179.1 4.9 %convolution_convert_fusion = bf16[512,1024]{1,0:T(8,128)(2,1)} fusion(bf16[256,1024]{1,0:T(8,128)(2,1)S(1)} %copy-done.7, bf16[512,256]{1,0:T(8,128)(2,1)S(1)} %fusion.28, bf16[15,256]{1,0:T(8,128)(2,1)S(1)} %collective-permute-done.1, bf16[15,256]{1,0:T(8,128)(2,1)S(1)} %collective-permute-done, f32[256]{0:T(256)S(1)} %copy-done.10, ...), kind=kOutput, calls=%fused_computation.67 | convolution fusion | flops 293732352 | bytes 1884160 | tf_op jit(solution)/shard_map/dot_general | solution.py:128
  184.0 26.0 %reduce-scatter.2.cloned.1.call-done = bf16[128,1024]{1,0:T(8,128)(2,1)} async-done(((bf16[512,1024]{1,0:T(8,128)(2,1)}), bf16[128,1024]{1,0:T(8,128)(2,1)}) %reduce-scatter.2.cloned.1.call-update) | async-done | bytes 262160 | tf_op jit(solution)/shard_map/reduce_scatter | solution.py:127
  209.9 1.7 add_convert_fusion
  (87 shorter events, 16.5 us)
Async XLA Ops:
  6.5 108.9 %copy-start = (bf16[256,1024]{1,0:T(8,128)(2,1)S(1)}, bf16[256,1024]{1,0:T(8,128)(2,1)}, u32[]{:S(2)}) copy-start(bf16[256,1024]{1,0:T(8,128)(2,1)} %param.21) | copy-start | bytes 1572868
  6.5 3.3 %copy-start.1 = (bf16[512,1024]{1,0:T(8,128)(2,1)S(1)}, bf16[512,1024]{1,0:T(8,128)(2,1)}, u32[]{:S(2)}) copy-start(bf16[512,1024]{1,0:T(8,128)(2,1)} %param.15) | copy-start | bytes 3145732
  6.5 3.3 %copy-start.5 = (bf16[1024,256]{1,0:T(8,128)(2,1)S(1)}, bf16[1024,256]{1,0:T(8,128)(2,1)}, u32[]{:S(2)}) copy-start(bf16[1024,256]{1,0:T(8,128)(2,1)} %param.19) | copy-start | bytes 1572868
  6.5 3.3 %copy-start.8 = (f32[1024]{0:T(1024)S(1)}, f32[1024]{0:T(1024)}, u32[]{:S(2)}) copy-start(f32[1024]{0:T(1024)} %param.17) | copy-start | bytes 12292
  6.5 35.4 %all-gather.4.cloned.1.call-start = ((), (), s32[]{:S(2)}) async-start(), calls=%async_computation.1 | async-start | bytes 1310720 | tf_op jit(solution)/shard_map/all_gather | solution.py:89
  9.8 1.4 copy-start.6
  11.1 1.4 copy-start.3
  11.1 59.8 %all-gather.6.cloned.1.call-start = ((), (), s32[]{:S(2)}) async-start(), calls=%async_computation.2 | async-start | bytes 1310720 | tf_op jit(solution)/shard_map/all_gather | solution.py:90
  12.4 155.9 %all-reduce.2.cloned.1.call-start = ((), (), s32[]{:S(2)}) async-start(), calls=%async_computation.3 | async-start | bytes 4194304 | tf_op jit(solution)/shard_map/psum | solution.py:111
  115.4 1.9 copy-start.2
  117.2 92.7 %reduce-scatter.2.cloned.1.call-start = ((), (), s32[]{:S(2)}) async-start(), calls=%async_computation.4 | async-start | bytes 1310720 | tf_op jit(solution)/shard_map/reduce_scatter | solution.py:127
  117.3 53.4 %copy-start.9 = (f32[1024]{0:T(1024)S(1)}, f32[1024]{0:T(1024)}, u32[]{:S(2)}) copy-start(f32[1024]{0:T(1024)} %param.22) | copy-start | bytes 12292
  168.3 2.4 %copy-start.4 = (bf16[2,1024,256]{2,1,0:T(8,128)(2,1)S(1)}, bf16[2,1024,256]{2,1,0:T(8,128)(2,1)}, u32[]{:S(2)}) copy-start(bf16[2,1024,256]{2,1,0:T(8,128)(2,1)} %param.23) | copy-start | bytes 3145732
  171.3 7.8 %copy-start.7 = (bf16[256,1024]{1,0:T(8,128)(2,1)S(1)}, bf16[256,1024]{1,0:T(8,128)(2,1)}, u32[]{:S(2)}) copy-start(bf16[256,1024]{1,0:T(8,128)(2,1)} %param.27) | copy-start | bytes 1572868
  171.3 7.8 %copy-start.10 = (f32[256]{0:T(256)S(1)}, f32[256]{0:T(256)}, u32[]{:S(2)}) copy-start(f32[256]{0:T(256)} %param.26) | copy-start | bytes 3076
  171.3 7.8 %copy-start.11 = (f32[256]{0:T(256)S(1)}, f32[256]{0:T(256)}, u32[]{:S(2)}) copy-start(f32[256]{0:T(256)} %param.25) | copy-start | bytes 3076
  171.9 5.9 %collective-permute-start.1 = (bf16[15,256]{1,0:T(8,128)(2,1)S(1)}, bf16[15,256]{1,0:T(8,128)(2,1)S(1)}, u32[]{:S(2)}, u32[]{:S(2)}) collective-permute-start(bf16[15,256]{1,0:T(8,128)(2,1)S(1)} %get-tuple-element.118), channel_id=1, source_target_pairs={{4,0},{8,4},{12,8},{5,1},{9,5},{13,9},{6,2},{10,6},{14,10},{7,3},{... | collective-permute-start | bytes 23048 | tf_op jit(solution)/shard_map/ppermute | solution.py:19
  173.2 5.9 %collective-permute-start = (bf16[15,256]{1,0:T(8,128)(2,1)S(1)}, bf16[15,256]{1,0:T(8,128)(2,1)S(1)}, u32[]{:S(2)}, u32[]{:S(2)}) collective-permute-start(bf16[15,256]{1,0:T(8,128)(2,1)S(1)} %get-tuple-element.117), channel_id=1, source_target_pairs={{0,4},{4,8},{8,12},{1,5},{5,9},{9,13},{2,6},{6,10},{10,14},{3,7},{... | collective-permute-start | bytes 23048 | tf_op jit(solution)/shard_map/ppermute | solution.py:16
Sparse Core Ops, SparseCore 0:
  11.2 30.6 all-gather.3
  43.5 27.3 all-gather.5
  117.4 50.8 all-reduce.1
  184.1 25.8 reduce-scatter.1
where the time goes:
time: 219 us; the launch traced here: 218 us
  waiting for transfers between devices  121 us (55%)
  matrix products  36.7 us (17%)
  other arithmetic  21.4 us (10%)
  blocking collectives  13.7 us (6%)
  between operations  13.4 us (6%)
  starting transfers between devices  6 us (3%)
  local copies, waits for them, and re-layouts  5.5 us (3%)
    psum x1, waiting for transfers between devices, local(): lax.psum(jnp.dot(attended, w_out, preferred_element_type=jnp.float32), 't...  50.9 us
    all_gather x1, waiting for transfers between devices, local(): val_part = lax.all_gather(vals, 'context', axis=0, tiled=True)  29 us
    reduce_scatter x1, waiting for transfers between devices, local(): lax.psum_scatter(jnp.dot(activated, w_point2, preferred_element_type=jnp....  26 us
    all_gather x1, waiting for transfers between devices, local(): key_part = lax.all_gather(keys, 'context', axis=0, tiled=True)  14 us
    all_gather x1, blocking collectives, local(): valid_part = lax.all_gather(frame_valid, 'context', axis=0, tiled=True)  13.7 us
    dot_general x4, matrix products, update(): jnp.einsum('hqk,khd->qhd', weights.astype(jnp.bfloat16), val_heads, prefe...  13.1 us
    reduce_sum x4, other arithmetic, update(): run_sum = run_sum * factor + jnp.sum(weights, axis=-1)  13.1 us
    dot_general x4, matrix products, update(): jnp.einsum('qhd,khd->hqk', query, key_heads, preferred_element_type=jnp.f...  11.6 us
  transfers between devices with their start and end apart: 6, of which 5 were waited for; matrix products, arithmetic and copies ran while one was open for 1% of the time, Pallas kernels for 0%

commit v1 on v0

--- a/solution.py
+++ b/solution.py
@@ -87,7 +87,29 @@
     )
     carry = start_state
     key_part = lax.all_gather(keys, "context", axis=0, tiled=True)
-    val_part = lax.all_gather(vals, "context", axis=0, tiled=True)
+    degree = jax.lax.psum(1, axis_name="context")
+    store = []
+    dev_j = 0
+    while dev_j < degree:
+        store.append((dev_j, (dev_j + 1) % degree))
+        dev_j = dev_j + 1
+    log = []
+    dev_j = 0
+    while dev_j < degree:
+        log.append((dev_j, (dev_j - 1) % degree))
+        dev_j += 1
+    a_now, mid_arr = ([vals], [vals])
+    for _ in range(degree // 2):
+        a_now.append(jax.lax.ppermute(a_now[-1], axis_name="context", perm=store))
+    q = 0
+    while q < (degree - 1) // 2:
+        mid_arr.append(jax.lax.ppermute(mid_arr[-1], axis_name="context", perm=log))
+        q = q + 1
+    val_part = jnp.roll(
+        jnp.concatenate([*a_now[::-1], *mid_arr[1:]], axis=0),
+        (jax.lax.axis_index("context") - degree // 2) * vals.shape[0],
+        axis=0,
+    )
     valid_part = lax.all_gather(frame_valid, "context", axis=0, tiled=True)
     rows = key_part.shape[0]
     shards = max(rows // frames, 1)

time: 219 us -> 199 us (0.909)
  waiting for transfers between devices: 121 us -> 89.3 us
  blocking collectives: 13.7 us -> 20.1 us
  starting transfers between devices: 6 us -> 11.2 us
    all_gather x1 -> x0, waiting for transfers between devices: 29 us -> none  [local(): val_part = lax.all_gather(vals, 'context', axis=0, tiled=True)]
    all_gather x1, waiting for transfers between devices: 14 us -> 0.01 us  [local(): key_part = lax.all_gather(keys, 'context', axis=0, tiled=True)]
    ppermute x0 -> x3, waiting for transfers between devices: none -> 11.2 us  [the longest x2 11.2 us: local(): a_now.append(jax.lax.ppermute(a_now[-1], axis_name='context', perm=store))]
    all_gather x1, blocking collectives: 13.7 us -> 20.1 us  [local(): valid_part = lax.all_gather(frame_valid, 'context', axis=0, tiled=True)]
    ppermute x0 -> x3, starting transfers between devices: none -> 5.29 us  [the longest x2 3.19 us: local(): a_now.append(jax.lax.ppermute(a_now[-1], axis_name='context', perm=store))]
  transfers between devices with their start and end apart: 6 -> 8, of which waited for: 5 -> 4; matrix products, arithmetic and copies ran while one was open for 1% -> 2% of each run, Pallas kernels for 0% -> 0%
where the time goes in v1:
time: 199 us
  waiting for transfers between devices  89.3 us (45%)
  matrix products  36 us (18%)
  other arithmetic  21.5 us (11%)
  blocking collectives  20.1 us (10%)
  between operations  13.4 us (7%)
  starting transfers between devices  11.2 us (6%)
  local copies, waits for them, and re-layouts  6.74 us (3%)
    psum x1, waiting for transfers between devices, local(): lax.psum(jnp.dot(attended, w_out, preferred_element_type=jnp.float32), 't...  50.7 us
    reduce_scatter x1, waiting for transfers between devices, local(): lax.psum_scatter(jnp.dot(activated, w_point2, preferred_element_type=jnp....  26 us
    all_gather x1, blocking collectives, local(): valid_part = lax.all_gather(frame_valid, 'context', axis=0, tiled=True)  20.1 us
    dot_general x4, matrix products, update(): jnp.einsum('hqk,khd->qhd', weights.astype(jnp.bfloat16), val_heads, prefe...  13.1 us
    reduce_sum x4, other arithmetic, update(): run_sum = run_sum * factor + jnp.sum(weights, axis=-1)  13.1 us
    dot_general x4, matrix products, update(): jnp.einsum('qhd,khd->hqk', query, key_heads, preferred_element_type=jnp.f...  11.6 us
    ppermute x2, waiting for transfers between devices, local(): a_now.append(jax.lax.ppermute(a_now[-1], axis_name='context', perm=store))  11.2 us
    dynamic_slice x12, local copies, waits for them, and re-layouts, local(): carry, unused = lax.scan(advance, carry, stacked)  5.39 us
  transfers between devices with their start and end apart: 8, of which 4 were waited for; matrix products, arithmetic and copies ran while one was open for 2% of the time, Pallas kernels for 0%

profile of v1, /device:TPU:0, one launch (start us, length us, event | category | flops | bytes accessed | tf_op | source)
XLA Modules:
  0.0 198.5 jit_solution(17826209684897552156)
XLA Ops:
  10.4 3.1 %collective-permute-start = (bf16[512,256]{1,0:T(8,128)(2,1)S(1)}, bf16[512,256]{1,0:T(8,128)(2,1)S(1)}, u32[]{:S(2)}, u32[]{:S(2)}) collective-permute-start(bf16[512,256]{1,0:T(8,128)(2,1)S(1)} %convolution_convert_fusion.1), channel_id=1, source_target_pairs={{0,4},{4,8},{8,12},{12,0},{1,5},{5,9},{9,13},{13,1},{2,6},{6,10},{... | collective-permute-start | bytes 786440 | tf_op jit(solution)/shard_map/ppermute | solution.py:103
  14.8 2.1 %collective-permute-start.2 = (bf16[512,256]{1,0:T(8,128)(2,1)S(1)}, bf16[512,256]{1,0:T(8,128)(2,1)S(1)}, u32[]{:S(2)}, u32[]{:S(2)}) collective-permute-start(bf16[512,256]{1,0:T(8,128)(2,1)S(1)} %convolution_convert_fusion.1), channel_id=1, source_target_pairs={{0,12},{4,0},{8,4},{12,8},{1,13},{5,1},{9,5},{13,9},{2,14},{6,2},{... | collective-permute-start | bytes 786440 | tf_op jit(solution)/shard_map/ppermute | solution.py:106
  16.9 20.1 %all-gather = s32[4,1,512]{2,1,0:T(1,128)S(1)} all-gather(s32[1,1,512]{2,1,0:T(1,128)S(1)} %bitcast.111), channel_id=1, replica_groups=mesh['groups'=2,'context'=4,'tensor'=4] {'context'}, dimensions={0}, use_global_device_ids=true | all-gather | bytes 10240 | tf_op jit(solution)/shard_map/all_gather | solution.py:113
  37.2 1.7 convolution_convert_fusion.2
  38.9 11.2 %collective-permute-done.1 = bf16[512,256]{1,0:T(8,128)(2,1)S(1)} collective-permute-done((bf16[512,256]{1,0:T(8,128)(2,1)S(1)}, bf16[512,256]{1,0:T(8,128)(2,1)S(1)}, u32[]{:S(2)}, u32[]{:S(2)}) %collective-permute-start.1) | collective-permute-done | bytes 262176 | tf_op jit(solution)/shard_map/ppermute | solution.py:103
  51.5 44.4 %while.15 = (s32[]{:T(128)}, f32[4,512]{1,0:T(4,128)S(1)}, f32[4,512]{1,0:T(4,128)S(1)}, f32[512,256]{0,1:T(8,128)S(1)}, s32[4,512]{1,0:T(4,128)S(1)}, /*index=5...) while((s32[]{:T(128)}, f32[4,512]{1,0:T(4,128)S(1)}, ...), condition=%wide.region_5.6_spmd.clone, body=%wide.region_2.5_spmd.clone.sunk | while | flops 282472960 | bytes 17698944 | solution.py:128
  52.7 2.9 %bitcast_reduce_fusion.2 = (f32[4,512]{1,0:T(4,128)S(1)}, f32[4,512,512]{2,1,0:T(8,128)}) fusion(pred[512]{0:T(512)(128)(4,1)S(1)} %compare_reduce_fusion.2, bf16[512,4,64]{0,2,1:T(8,128)(2,1)S(1)} %bitcast.104, bf16[512,4,64]{0,2,1:T(8,128)(2,1)S(1)} %get-tuple-element.245), kind=kOutput, calls=%fused_computation.1.clone.1 | convolution fusion | flops 137361408 | bytes 4727296 | tf_op jit(solution)/shard_map/while/body/eval_jaxpr/qhd,khd->hqk/dot_general | solution.py:63
  55.6 3.3 %fusion.96 = f32[4,512]{1,0:T(4,128)S(1)} fusion(f32[4,512,512]{2,1,0:T(8,128)} %get-tuple-element.216, f32[4,512]{1,0:T(4,128)S(1)} %get-tuple-element.240, pred[512]{0:T(512)(128)(4,1)S(1)} %compare_reduce_fusion.2), kind=kLoop, calls=%fused_computation.6.clone.1 | loop fusion | flops 5240832 | bytes 4211200 | tf_op jit(solution)/shard_map/while/body/eval_jaxpr/reduce_sum | solution.py:70
  59.1 3.3 %fusion.98 = f32[4,64,512]{2,1,0:T(8,128)S(1)} fusion(bf16[512,4,64]{0,2,1:T(8,128)(2,1)S(1)} %bitcast.106, f32[4,512,512]{2,1,0:T(8,128)} %get-tuple-element.216, f32[4,512]{1,0:T(4,128)S(1)} %get-tuple-element.240, pred[512]{0:T(512)(128)(4,1)S(1)} %compare_reduce_fusion.2), kind=kOutput, calls=%fused_computation.7.clone.1 | convolution fusion | flops 139460608 | bytes 4989440 | tf_op jit(solution)/shard_map/while/body/eval_jaxpr/hqk,khd->qhd/dot_general | solution.py:71
  63.8 2.9 %bitcast_reduce_fusion.2 = (f32[4,512]{1,0:T(4,128)S(1)}, f32[4,512,512]{2,1,0:T(8,128)}) fusion(pred[512]{0:T(512)(128)(4,1)S(1)} %compare_reduce_fusion.2, bf16[512,4,64]{0,2,1:T(8,128)(2,1)S(1)} %bitcast.104, bf16[512,4,64]{0,2,1:T(8,128)(2,1)S(1)} %get-tuple-element.245), kind=kOutput, calls=%fused_computation.1.clone.1 | convolution fusion | flops 137361408 | bytes 4727296 | tf_op jit(solution)/shard_map/while/body/eval_jaxpr/qhd,khd->hqk/dot_general | solution.py:63
  66.7 3.3 %fusion.96 = f32[4,512]{1,0:T(4,128)S(1)} fusion(f32[4,512,512]{2,1,0:T(8,128)} %get-tuple-element.216, f32[4,512]{1,0:T(4,128)S(1)} %get-tuple-element.240, pred[512]{0:T(512)(128)(4,1)S(1)} %compare_reduce_fusion.2), kind=kLoop, calls=%fused_computation.6.clone.1 | loop fusion | flops 5240832 | bytes 4211200 | tf_op jit(solution)/shard_map/while/body/eval_jaxpr/reduce_sum | solution.py:70
  70.2 3.3 %fusion.98 = f32[4,64,512]{2,1,0:T(8,128)S(1)} fusion(bf16[512,4,64]{0,2,1:T(8,128)(2,1)S(1)} %bitcast.106, f32[4,512,512]{2,1,0:T(8,128)} %get-tuple-element.216, f32[4,512]{1,0:T(4,128)S(1)} %get-tuple-element.240, pred[512]{0:T(512)(128)(4,1)S(1)} %compare_reduce_fusion.2), kind=kOutput, calls=%fused_computation.7.clone.1 | convolution fusion | flops 139460608 | bytes 4989440 | tf_op jit(solution)/shard_map/while/body/eval_jaxpr/hqk,khd->qhd/dot_general | solution.py:71
  74.9 2.9 %bitcast_reduce_fusion.2 = (f32[4,512]{1,0:T(4,128)S(1)}, f32[4,512,512]{2,1,0:T(8,128)}) fusion(pred[512]{0:T(512)(128)(4,1)S(1)} %compare_reduce_fusion.2, bf16[512,4,64]{0,2,1:T(8,128)(2,1)S(1)} %bitcast.104, bf16[512,4,64]{0,2,1:T(8,128)(2,1)S(1)} %get-tuple-element.245), kind=kOutput, calls=%fused_computation.1.clone.1 | convolution fusion | flops 137361408 | bytes 4727296 | tf_op jit(solution)/shard_map/while/body/eval_jaxpr/qhd,khd->hqk/dot_general | solution.py:63
  77.9 3.3 %fusion.96 = f32[4,512]{1,0:T(4,128)S(1)} fusion(f32[4,512,512]{2,1,0:T(8,128)} %get-tuple-element.216, f32[4,512]{1,0:T(4,128)S(1)} %get-tuple-element.240, pred[512]{0:T(512)(128)(4,1)S(1)} %compare_reduce_fusion.2), kind=kLoop, calls=%fused_computation.6.clone.1 | loop fusion | flops 5240832 | bytes 4211200 | tf_op jit(solution)/shard_map/while/body/eval_jaxpr/reduce_sum | solution.py:70
  81.3 3.3 %fusion.98 = f32[4,64,512]{2,1,0:T(8,128)S(1)} fusion(bf16[512,4,64]{0,2,1:T(8,128)(2,1)S(1)} %bitcast.106, f32[4,512,512]{2,1,0:T(8,128)} %get-tuple-element.216, f32[4,512]{1,0:T(4,128)S(1)} %get-tuple-element.240, pred[512]{0:T(512)(128)(4,1)S(1)} %compare_reduce_fusion.2), kind=kOutput, calls=%fused_computation.7.clone.1 | convolution fusion | flops 139460608 | bytes 4989440 | tf_op jit(solution)/shard_map/while/body/eval_jaxpr/hqk,khd->qhd/dot_general | solution.py:71
  86.0 2.9 %bitcast_reduce_fusion.2 = (f32[4,512]{1,0:T(4,128)S(1)}, f32[4,512,512]{2,1,0:T(8,128)}) fusion(pred[512]{0:T(512)(128)(4,1)S(1)} %compare_reduce_fusion.2, bf16[512,4,64]{0,2,1:T(8,128)(2,1)S(1)} %bitcast.104, bf16[512,4,64]{0,2,1:T(8,128)(2,1)S(1)} %get-tuple-element.245), kind=kOutput, calls=%fused_computation.1.clone.1 | convolution fusion | flops 137361408 | bytes 4727296 | tf_op jit(solution)/shard_map/while/body/eval_jaxpr/qhd,khd->hqk/dot_general | solution.py:63
  89.0 3.3 %fusion.96 = f32[4,512]{1,0:T(4,128)S(1)} fusion(f32[4,512,512]{2,1,0:T(8,128)} %get-tuple-element.216, f32[4,512]{1,0:T(4,128)S(1)} %get-tuple-element.240, pred[512]{0:T(512)(128)(4,1)S(1)} %compare_reduce_fusion.2), kind=kLoop, calls=%fused_computation.6.clone.1 | loop fusion | flops 5240832 | bytes 4211200 | tf_op jit(solution)/shard_map/while/body/eval_jaxpr/reduce_sum | solution.py:70
  92.4 3.3 %fusion.98 = f32[4,64,512]{2,1,0:T(8,128)S(1)} fusion(bf16[512,4,64]{0,2,1:T(8,128)(2,1)S(1)} %bitcast.106, f32[4,512,512]{2,1,0:T(8,128)} %get-tuple-element.216, f32[4,512]{1,0:T(4,128)S(1)} %get-tuple-element.240, pred[512]{0:T(512)(128)(4,1)S(1)} %compare_reduce_fusion.2), kind=kOutput, calls=%fused_computation.7.clone.1 | convolution fusion | flops 139460608 | bytes 4989440 | tf_op jit(solution)/shard_map/while/body/eval_jaxpr/hqk,khd->qhd/dot_general | solution.py:71
  96.0 1.8 fusion.73
  97.9 50.7 %all-reduce.2.cloned.1.call-done = f32[512,1024]{1,0:T(8,128)} async-done(((f32[512,1024]{1,0:T(8,128)}), f32[512,1024]{1,0:T(8,128)}) %all-reduce.2.cloned.1.call-update) | async-done | bytes 2097168 | tf_op jit(solution)/shard_map/psum | solution.py:133
  148.6 2.0 %convert_reduce_fusion.1 = (f32[512]{0:T(512)S(1)}, bf16[512,1024]{1,0:T(8,128)(2,1)S(1)}) fusion(f32[512,1024]{1,0:T(8,128)} %all-reduce.2.cloned.1.call-done, bf16[512,1024]{1,0:T(8,128)(2,1)S(1)} %copy-done.1), kind=kLoop, calls=%fused_computation.27 | loop fusion | flops 2620928 | bytes 4196352 | tf_op jit(solution)/shard_map/reduce_sum | solution.py:26
  153.5 4.5 %collective-permute-start.3 = (bf16[15,256]{1,0:T(8,128)(2,1)S(1)}, bf16[15,256]{1,0:T(8,128)(2,1)S(1)}, u32[]{:S(2)}, u32[]{:S(2)}) collective-permute-start(bf16[15,256]{1,0:T(8,128)(2,1)S(1)} %get-tuple-element.125), channel_id=1, source_target_pairs={{0,4},{4,8},{8,12},{1,5},{5,9},{9,13},{2,6},{6,10},{10,14},{3,7},{... | collective-permute-start | bytes 23048 | tf_op jit(solution)/shard_map/ppermute | solution.py:16
  159.4 4.9 %convolution_convert_fusion = bf16[512,1024]{1,0:T(8,128)(2,1)} fusion(bf16[256,1024]{1,0:T(8,128)(2,1)S(1)} %copy-done.7, bf16[512,256]{1,0:T(8,128)(2,1)S(1)} %fusion.28, bf16[15,256]{1,0:T(8,128)(2,1)S(1)} %collective-permute-done.4, bf16[15,256]{1,0:T(8,128)(2,1)S(1)} %collective-permute-done.3, f32[256]{0:T(256)S(1)} %copy-done.10, ...), kind=kOutput, calls=%fused_computation.67 | convolution fusion | flops 293732352 | bytes 1884160 | tf_op jit(solution)/shard_map/dot_general | solution.py:150
  164.3 26.0 %reduce-scatter.2.cloned.1.call-done = bf16[128,1024]{1,0:T(8,128)(2,1)} async-done(((bf16[512,1024]{1,0:T(8,128)(2,1)}), bf16[128,1024]{1,0:T(8,128)(2,1)}) %reduce-scatter.2.cloned.1.call-update) | async-done | bytes 262160 | tf_op jit(solution)/shard_map/reduce_scatter | solution.py:149
  (99 shorter events, 18.9 us)
Async XLA Ops:
  6.5 89.4 %copy-start = (bf16[256,1024]{1,0:T(8,128)(2,1)S(1)}, bf16[256,1024]{1,0:T(8,128)(2,1)}, u32[]{:S(2)}) copy-start(bf16[256,1024]{1,0:T(8,128)(2,1)} %param.21) | copy-start | bytes 1572868
  6.5 3.3 %copy-start.1 = (bf16[512,1024]{1,0:T(8,128)(2,1)S(1)}, bf16[512,1024]{1,0:T(8,128)(2,1)}, u32[]{:S(2)}) copy-start(bf16[512,1024]{1,0:T(8,128)(2,1)} %param.15) | copy-start | bytes 3145732
  6.5 3.4 %copy-start.8 = (f32[1024]{0:T(1024)S(1)}, f32[1024]{0:T(1024)}, u32[]{:S(2)}) copy-start(f32[1024]{0:T(1024)} %param.17) | copy-start | bytes 12292
  6.5 3.4 %copy-start.5 = (bf16[1024,256]{1,0:T(8,128)(2,1)S(1)}, bf16[1024,256]{1,0:T(8,128)(2,1)}, u32[]{:S(2)}) copy-start(bf16[1024,256]{1,0:T(8,128)(2,1)} %param.20) | copy-start | bytes 1572868
  6.5 44.9 %all-gather.3.cloned.1.call-start = ((), (), s32[]{:S(2)}) async-start(), calls=%async_computation.1 | async-start | bytes 1310720 | tf_op jit(solution)/shard_map/all_gather | solution.py:89
  8.2 5.4 %copy-start.6 = (bf16[1024,256]{1,0:T(8,128)(2,1)S(1)}, bf16[1024,256]{1,0:T(8,128)(2,1)}, u32[]{:S(2)}) copy-start(bf16[1024,256]{1,0:T(8,128)(2,1)} %param.19) | copy-start | bytes 1572868
  10.4 6.5 %copy-start.3 = (s32[512]{0:T(512)S(1)}, s32[512]{0:T(512)}, u32[]{:S(2)}) copy-start(s32[512]{0:T(512)} %param.16) | copy-start | bytes 6148
  10.4 26.6 %collective-permute-start = (bf16[512,256]{1,0:T(8,128)(2,1)S(1)}, bf16[512,256]{1,0:T(8,128)(2,1)S(1)}, u32[]{:S(2)}, u32[]{:S(2)}) collective-permute-start(bf16[512,256]{1,0:T(8,128)(2,1)S(1)} %convolution_convert_fusion.1), channel_id=1, source_target_pairs={{0,4},{4,8},{8,12},{12,0},{1,5},{5,9},{9,13},{13,1},{2,6},{6,10},{... | collective-permute-start | bytes 786440 | tf_op jit(solution)/shard_map/ppermute | solution.py:103
  14.8 133.8 %all-reduce.2.cloned.1.call-start = ((), (), s32[]{:S(2)}) async-start(), calls=%async_computation.2 | async-start | bytes 4194304 | tf_op jit(solution)/shard_map/psum | solution.py:133
  14.8 35.4 %collective-permute-start.2 = (bf16[512,256]{1,0:T(8,128)(2,1)S(1)}, bf16[512,256]{1,0:T(8,128)(2,1)S(1)}, u32[]{:S(2)}, u32[]{:S(2)}) collective-permute-start(bf16[512,256]{1,0:T(8,128)(2,1)S(1)} %convolution_convert_fusion.1), channel_id=1, source_target_pairs={{0,12},{4,0},{8,4},{12,8},{1,13},{5,1},{9,5},{13,9},{2,14},{6,2},{... | collective-permute-start | bytes 786440 | tf_op jit(solution)/shard_map/ppermute | solution.py:106
  37.1 13.1 %collective-permute-start.1 = (bf16[512,256]{1,0:T(8,128)(2,1)S(1)}, bf16[512,256]{1,0:T(8,128)(2,1)S(1)}, u32[]{:S(2)}, u32[]{:S(2)}) collective-permute-start(bf16[512,256]{1,0:T(8,128)(2,1)S(1)} %collective-permute-done), channel_id=1, source_target_pairs={{0,4},{4,8},{8,12},{12,0},{1,5},{5,9},{9,13},{13,1},{2,6},{6,10},{... | collective-permute-start | bytes 786440 | tf_op jit(solution)/shard_map/ppermute | solution.py:103
  96.0 1.9 copy-start.2
  97.8 92.5 %reduce-scatter.2.cloned.1.call-start = ((), (), s32[]{:S(2)}) async-start(), calls=%async_computation.3 | async-start | bytes 1310720 | tf_op jit(solution)/shard_map/reduce_scatter | solution.py:149
  97.9 53.2 %copy-start.9 = (f32[1024]{0:T(1024)S(1)}, f32[1024]{0:T(1024)}, u32[]{:S(2)}) copy-start(f32[1024]{0:T(1024)} %param.22) | copy-start | bytes 12292
  148.6 2.4 %copy-start.4 = (bf16[2,1024,256]{2,1,0:T(8,128)(2,1)S(1)}, bf16[2,1024,256]{2,1,0:T(8,128)(2,1)}, u32[]{:S(2)}) copy-start(bf16[2,1024,256]{2,1,0:T(8,128)(2,1)} %param.23) | copy-start | bytes 3145732
  151.6 7.8 %copy-start.7 = (bf16[256,1024]{1,0:T(8,128)(2,1)S(1)}, bf16[256,1024]{1,0:T(8,128)(2,1)}, u32[]{:S(2)}) copy-start(bf16[256,1024]{1,0:T(8,128)(2,1)} %param.27) | copy-start | bytes 1572868
  151.6 7.8 %copy-start.10 = (f32[256]{0:T(256)S(1)}, f32[256]{0:T(256)}, u32[]{:S(2)}) copy-start(f32[256]{0:T(256)} %param.26) | copy-start | bytes 3076
  151.6 7.8 %copy-start.11 = (f32[256]{0:T(256)S(1)}, f32[256]{0:T(256)}, u32[]{:S(2)}) copy-start(f32[256]{0:T(256)} %param.25) | copy-start | bytes 3076
  152.2 5.9 %collective-permute-start.4 = (bf16[15,256]{1,0:T(8,128)(2,1)S(1)}, bf16[15,256]{1,0:T(8,128)(2,1)S(1)}, u32[]{:S(2)}, u32[]{:S(2)}) collective-permute-start(bf16[15,256]{1,0:T(8,128)(2,1)S(1)} %get-tuple-element.126), channel_id=1, source_target_pairs={{4,0},{8,4},{12,8},{5,1},{9,5},{13,9},{6,2},{10,6},{14,10},{7,3},{... | collective-permute-start | bytes 23048 | tf_op jit(solution)/shard_map/ppermute | solution.py:19
  153.5 5.9 %collective-permute-start.3 = (bf16[15,256]{1,0:T(8,128)(2,1)S(1)}, bf16[15,256]{1,0:T(8,128)(2,1)S(1)}, u32[]{:S(2)}, u32[]{:S(2)}) collective-permute-start(bf16[15,256]{1,0:T(8,128)(2,1)S(1)} %get-tuple-element.125), channel_id=1, source_target_pairs={{0,4},{4,8},{8,12},{1,5},{5,9},{9,13},{2,6},{6,10},{10,14},{3,7},{... | collective-permute-start | bytes 23048 | tf_op jit(solution)/shard_map/ppermute | solution.py:16
Sparse Core Ops, SparseCore 0:
  14.9 33.2 all-gather.2
  97.9 50.6 all-reduce.1
  164.4 25.8 reduce-scatter.1
